TPU v7x, 128 devices: a whole 4x4x4 slice. The times are simulated.
128 devices in a mesh: seq: 16 (over x, z), head: 8 (over y, core).
Axes of the slice: x: 4, y: 4, z: 4, core: 2. Of those that a mesh axis runs over, the one named last changes fastest.
Arguments:
- queries: bfloat16 [65536, 16, 128], P(('seq', 'head'))
- keys: bfloat16 [65536, 4, 128], P('seq')
- values: bfloat16 [65536, 4, 128], P('seq')
- refine_owner: int32 [512, 4], P('seq'), may hold values from 0 to 15, all different within a row; in each aligned block of 32 rows (0 to 31, 32 to 63, ...) at most 16 rows name the same one
- refine_local: int32 [512, 4], P('seq'), may hold values from 0 to 31
Outputs:
- attended: bfloat16 [65536, 16, 128], P('seq', 'head')
Inputs may be any that keep to these rules, and one draw needn't show every extreme that they name: `refine_owner`: in each row the 4 entries differ. In the rows of one device (aligned blocks of 32 rows) no value is named more than 16 times.
All inputs are finite; a program needn't handle non-finite values.
Results may differ from a plain program's by a relative error of at most 0.008.
Values may be sent and summed in bfloat16 or wider, within the bound.
A program may use at most 128 MiB of HBM per device.

v0:
```python
import math

import jax
import jax.numpy as jnp
from jax import lax
from jax.sharding import PartitionSpec as P

BLK = 128


def on_device(queries, keys, values, refine_owner, refine_local):
    seq_count = lax.axis_size("seq")
    local_queries = lax.all_to_all(queries, "head", split_axis=1, concat_axis=0, tiled=True)
    tok_rows, head_local, head_dim = local_queries.shape
    kv_heads = keys.shape[1]
    group_size = head_local * lax.axis_size("head") // kv_heads
    kv_index = lax.axis_index("head") * head_local // group_size
    key_own = lax.dynamic_index_in_dim(keys, kv_index, 1, keepdims=False)
    value_own = lax.dynamic_index_in_dim(values, kv_index, 1, keepdims=False)
    blocks_dev = tok_rows // BLK
    ref_count = refine_owner.shape[1]
    key_blocks = key_own.reshape(blocks_dev, BLK, head_dim)
    value_blocks = value_own.reshape(blocks_dev, BLK, head_dim)
    targets = refine_owner * blocks_dev + refine_local
    key_mean = jnp.mean(key_blocks, axis=1, dtype=jnp.float32).astype(jnp.bfloat16)
    value_mean = jnp.mean(value_blocks, axis=1, dtype=jnp.float32).astype(jnp.bfloat16)
    key_means, value_means = (
        lax.all_gather(key_mean, "seq", axis=0, tiled=True),
        lax.all_gather(value_mean, "seq", axis=0, tiled=True),
    )
    owner_flat = refine_owner.reshape(-1)
    local_flat = refine_local.reshape(-1)
    one_hot = (owner_flat[:, None] == jnp.arange(seq_count, dtype=jnp.int32)[None, :]).astype(
        jnp.int32
    )
    slot_index = jnp.sum((jnp.cumsum(one_hot, axis=0) - 1) * one_hot, axis=1)
    capacity = 2 * blocks_dev * ref_count // seq_count
    send_table = (
        jnp.zeros((seq_count, capacity), jnp.int32).at[owner_flat, slot_index].set(local_flat)
    )
    wanted = lax.all_to_all(send_table, "seq", split_axis=0, concat_axis=0, tiled=True)
    picked_keys = key_blocks[wanted]
    picked_values = value_blocks[wanted]
    arrived_keys, arrived_values = (
        lax.all_to_all(picked_keys, "seq", split_axis=0, concat_axis=0, tiled=True),
        lax.all_to_all(picked_values, "seq", split_axis=0, concat_axis=0, tiled=True),
    )
    position = owner_flat * capacity + slot_index
    far_keys = arrived_keys.reshape(-1, BLK, head_dim)[position].reshape(
        blocks_dev, ref_count, BLK, head_dim
    )
    far_values = arrived_values.reshape(-1, BLK, head_dim)[position].reshape(
        blocks_dev, ref_count, BLK, head_dim
    )
    total_blocks = key_means.shape[0]
    fine_keys = jnp.concatenate([key_blocks[:, None], far_keys], axis=1)
    fine_values = jnp.concatenate([value_blocks[:, None], far_values], axis=1)
    first_block = lax.axis_index("seq") * blocks_dev
    own_ids = (first_block + jnp.arange(blocks_dev, dtype=jnp.int32))[:, None]
    block_ids = jnp.concatenate([own_ids, targets], axis=1)
    key_means_f = key_means.astype(jnp.float32)
    block_iota = jnp.arange(total_blocks, dtype=jnp.int32)
    score_scale = head_dim ** (-0.5)
    per_step = min(blocks_dev, max(1, 512 // BLK))
    step_count = blocks_dev // per_step
    listed = ref_count + 1

    def attend_group(packed):
        query_part, keys_part, values_part, ids_part = packed
        query_means = jnp.mean(query_part, axis=1, dtype=jnp.float32)
        coarse = jnp.einsum(
            "ghd,jd->ghj", query_means, key_means_f, precision=lax.Precision.HIGHEST
        ) * score_scale + math.log(BLK)
        excluded = jnp.any(ids_part[:, :, None] == block_iota[None, None, :], axis=1)
        coarse = jnp.where(excluded[:, None, :], -1e30, coarse)
        keys_flat = keys_part.reshape(per_step, listed * BLK, head_dim)
        values_flat = values_part.reshape(per_step, listed * BLK, head_dim)
        fine = (
            jnp.einsum("gthd,gud->gthu", query_part, keys_flat, preferred_element_type=jnp.float32)
            * score_scale
        )
        row_max = jnp.maximum(jnp.max(coarse, axis=-1)[:, None, :], jnp.max(fine, axis=-1))
        coarse_weights = jnp.where(
            excluded[:, None, None, :], 0.0, jnp.exp(coarse[:, None] - row_max[..., None])
        )
        fine_weights = jnp.exp(fine - row_max[..., None])
        normaliser = jnp.sum(coarse_weights, axis=-1) + jnp.sum(fine_weights, axis=-1)
        weighted = jnp.einsum(
            "gthj,jd->gthd",
            coarse_weights.astype(jnp.bfloat16),
            value_means,
            preferred_element_type=jnp.float32,
        )
        weighted = weighted + jnp.einsum(
            "gthu,gud->gthd",
            fine_weights.astype(jnp.bfloat16),
            values_flat,
            preferred_element_type=jnp.float32,
        )
        return (weighted / normaliser[..., None]).astype(jnp.bfloat16)

    packed = (
        local_queries.reshape(step_count, per_step, BLK, head_local, head_dim),
        fine_keys.reshape(step_count, per_step, listed, BLK, head_dim),
        fine_values.reshape(step_count, per_step, listed, BLK, head_dim),
        block_ids.reshape(step_count, per_step, listed),
    )
    attended = lax.map(attend_group, packed)
    return attended.reshape(tok_rows, head_local, head_dim)


def solution(mesh):
    return jax.shard_map(
        on_device,
        mesh=mesh,
        in_specs=(
            P(("seq", "head"), None, None),
            P("seq", None, None),
            P("seq", None, None),
            P("seq", None),
            P("seq", None),
        ),
        out_specs=P("seq", "head", None),
        check_vma=False,
    )
```

profile of v0, /device:TPU:10, one launch (start us, length us, event | category | flops | bytes accessed | tf_op | source)
XLA Modules:
  0.0 446.2 jit_solution(9402142178831841110)
XLA Ops:
  2.9 17.8 %scatter_fusion = s32[16,16]{1,0:T(8,128)} fusion(s32[16,16]{1,0:T(8,128)} %broadcast.130, s32[128]{0:T(128)S(1)} %get-tuple-element.134, s32[128]{0:T(128)S(1)} %reshape.224), kind=kCustom, calls=%fused_computation.4 | custom fusion | bytes 2560 | tf_op jit(solution)/shard_map/scatter | solution.py:39
  20.7 8.3 %all-to-all-start.1 = ((s32[16,1,16]{2,1,0:T(1,128)}), s32[16,1,16]{2,1,0:T(1,128)S(1)}, u32[]{:S(2)}, u32[]{:S(2)}) async-start(s32[16,1,16]{2,1,0:T(1,128)} %bitcast.9), calls=%async_computation.1 | async-start | bytes 16384 | tf_op jit(solution)/shard_map/all_to_all | solution.py:41
  29.0 7.5 %constant_dynamic-slice_fusion.3 = (bf16[4096,1,128]{2,1,0:T(2,128)(2,1)S(1)}, bf16[4096,1,128]{2,1,0:T(2,128)(2,1)}) fusion(bf16[4096,4,128]{2,1,0:T(4,128)(2,1)} %param.9, s32[]{:T(128)S(6)} %select_n.61, bf16[4096,4,128]{2,1,0:T(4,128)(2,1)} %param.8), kind=kLoop, calls=%fused_computation.69 | loop fusion | bytes 4194308 | tf_op jit(solution)/shard_map/jit(dynamic_index_in_dim)/dynamic_slice | solution.py:19
  36.7 8.3 %gather_fusion.2 = bf16[256,128,128]{2,1,0:T(8,128)(2,1)} fusion(bf16[32,128,128]{2,1,0:T(8,128)(2,1)S(1)} %bitcast.92, s32[1024]{0:T(1024)S(1)} %pad_clamp_fusion.1), kind=kCustom, calls=%fused_computation.2 | custom fusion | bytes 16778240 | tf_op jit(solution)/shard_map/gather | solution.py:43
  45.1 7.4 %all-to-all-start.3 = ((bf16[16,16,128,128]{3,2,1,0:T(8,128)(2,1)}), bf16[16,16,128,128]{3,2,1,0:T(8,128)(2,1)}, u32[]{:S(2)}, u32[]{:S(2)}) async-start(bf16[16,16,128,128]{3,2,1,0:T(8,128)(2,1)} %bitcast.101), calls=%async_computation.3 | async-start | bytes 16777216 | tf_op jit(solution)/shard_map/all_to_all | solution.py:46
  52.5 1.7 copy.77
  54.2 8.4 %gather_fusion = bf16[256,128,128]{2,1,0:T(8,128)(2,1)} fusion(bf16[32,128,128]{2,1,0:T(8,128)(2,1)S(1)} %bitcast.95, s32[1024]{0:T(1024)S(1)} %pad_clamp_fusion.1), kind=kCustom, calls=%fused_computation | custom fusion | bytes 16778240 | tf_op jit(solution)/shard_map/gather | solution.py:42
  62.6 93.9 %all-to-all-done.3 = bf16[16,16,128,128]{3,2,1,0:T(8,128)(2,1)} async-done(((bf16[16,16,128,128]{3,2,1,0:T(8,128)(2,1)}), bf16[16,16,128,128]{3,2,1,0:T(8,128)(2,1)}, u32[]{:S(2)}, u32[]{:S(2)}) %all-to-all-start.3) | async-done | bytes 8388640 | tf_op jit(solution)/shard_map/all_to_all | solution.py:46
  156.5 45.9 %all-to-all-start.2 = ((bf16[16,16,128,128]{3,2,1,0:T(8,128)(2,1)}), bf16[16,16,128,128]{3,2,1,0:T(8,128)(2,1)}, u32[]{:S(2)}, u32[]{:S(2)}) async-start(bf16[16,16,128,128]{3,2,1,0:T(8,128)(2,1)} %bitcast.100), calls=%async_computation.2 | async-start | bytes 16777216 | tf_op jit(solution)/shard_map/all_to_all | solution.py:45
  202.4 3.4 copy.59
  205.9 94.1 %all-to-all-done.2 = bf16[16,16,128,128]{3,2,1,0:T(8,128)(2,1)} async-done(((bf16[16,16,128,128]{3,2,1,0:T(8,128)(2,1)}), bf16[16,16,128,128]{3,2,1,0:T(8,128)(2,1)}, u32[]{:S(2)}, u32[]{:S(2)}) %all-to-all-start.2) | async-done | bytes 8388640 | tf_op jit(solution)/shard_map/all_to_all | solution.py:45
  300.0 4.9 %all-to-all-start = ((bf16[512,16,128]{2,0,1:T(8,128)(2,1)}), bf16[512,16,128]{2,0,1:T(8,128)(2,1)}, u32[]{:S(2)}, u32[]{:S(2)}) async-start(bf16[512,16,128]{2,0,1:T(8,128)(2,1)} %copy.59), calls=%async_computation | async-start | bytes 4194304 | tf_op jit(solution)/shard_map/all_to_all | solution.py:13
  305.1 28.6 %all_gather.6 = bf16[512,128]{1,0:T(8,128)(2,1)S(1)} all-gather(bf16[32,128]{1,0:T(8,128)(2,1)S(1)} %multiply_convert_fusion.1), channel_id=1, replica_groups=mesh['seq'=16,'head'=8] {'seq'}, dimensions={0}, use_global_device_ids=true | all-gather | bytes 139264 | tf_op jit(solution)/shard_map/all_gather | solution.py:28
  334.2 24.0 %all_gather.7 = bf16[512,128]{1,0:T(8,128)(2,1)S(1)} all-gather(bf16[32,128]{1,0:T(8,128)(2,1)S(1)} %multiply_convert_fusion), channel_id=1, replica_groups=mesh['seq'=16,'head'=8] {'seq'}, dimensions={0}, use_global_device_ids=true | all-gather | bytes 139264 | tf_op jit(solution)/shard_map/all_gather | solution.py:29
  358.2 6.4 %gather_fusion.3 = bf16[128,128,128]{2,1,0:T(8,128)(2,1)} fusion(bf16[256,128,128]{2,1,0:T(8,128)(2,1)} %bitcast.19, s32[1024]{0:T(1024)S(1)} %pad_clamp_fusion), kind=kCustom, calls=%fused_computation.3 | custom fusion | bytes 8389120 | tf_op jit(solution)/shard_map/gather | solution.py:52
  364.6 6.4 %gather_fusion.1 = bf16[128,128,128]{2,1,0:T(8,128)(2,1)} fusion(bf16[256,128,128]{2,1,0:T(8,128)(2,1)} %bitcast.12, s32[1024]{0:T(1024)S(1)} %pad_clamp_fusion), kind=kCustom, calls=%fused_computation.1 | custom fusion | bytes 8389120 | tf_op jit(solution)/shard_map/gather | solution.py:49
  371.0 5.1 %pad_maximum_fusion.1 = bf16[8,4,5,128,128]{4,3,2,1,0:T(8,128)(2,1)} fusion(bf16[8,4,4,128,128]{4,3,2,1,0:T(8,128)(2,1)} %bitcast.103, bf16[8,4,1,128,128]{4,3,2,1,0:T(8,128)(2,1)S(1)} %bitcast.94), kind=kLoop, calls=%fused_computation.46 | loop fusion | flops 2621440 | bytes 10485760 | tf_op jit(solution)/shard_map/concatenate | solution.py:57
  376.1 2.8 pad_maximum_fusion
  378.9 67.2 %while.11 = (s32[]{:T(128)}, bf16[8,4,128,2,128]{4,3,2,1,0:T(2,128)(2,1)}, s32[8,4,5]{2,1,0:T(4,128)S(1)}, bf16[8,4,128,2,128]{4,2,1,3,0:T(8,128)(2,1)}, f32[512...) while((s32[]{:T(128)}, ...), condition=%wide.region_12.13_spmd.clone, body=%wide.region_5.12_spmd.clone.sunk | while | flops 485131264 | bytes 14702709 | solution.py:108
  379.1 1.0 convert_reduce_fusion.4
  380.6 1.4 constant_dynamic-slice_fusion.13
  382.0 1.6 multiply_reduce_fusion.2
  386.3 1.0 copy_dynamic-update-slice_fusion.2
  387.5 1.0 convert_reduce_fusion.4
  389.0 1.4 constant_dynamic-slice_fusion.13
  390.4 1.6 multiply_reduce_fusion.2
  394.7 1.0 copy_dynamic-update-slice_fusion.2
  395.9 1.0 convert_reduce_fusion.4
  397.4 1.4 constant_dynamic-slice_fusion.13
  398.8 1.6 multiply_reduce_fusion.2
  404.3 1.0 convert_reduce_fusion.4
  405.8 1.4 constant_dynamic-slice_fusion.13
  407.2 1.6 multiply_reduce_fusion.2
  411.6 1.0 copy_dynamic-update-slice_fusion.2
  412.7 1.0 convert_reduce_fusion.4
  414.2 1.4 constant_dynamic-slice_fusion.13
  415.6 1.6 multiply_reduce_fusion.2
  421.1 1.0 convert_reduce_fusion.4
  422.6 1.4 constant_dynamic-slice_fusion.13
  424.1 1.6 multiply_reduce_fusion.2
  428.4 1.0 copy_dynamic-update-slice_fusion.2
  429.5 1.0 convert_reduce_fusion.4
  431.0 1.4 constant_dynamic-slice_fusion.13
  432.5 1.6 multiply_reduce_fusion.2
  437.9 1.0 convert_reduce_fusion.4
  439.5 1.4 constant_dynamic-slice_fusion.13
  440.9 1.6 multiply_reduce_fusion.2
  445.2 1.0 copy_dynamic-update-slice_fusion.2
  (133 shorter events, 34.1 us)
Async XLA Ops:
  20.7 15.9 %all-to-all-start.1 = ((s32[16,1,16]{2,1,0:T(1,128)}), s32[16,1,16]{2,1,0:T(1,128)S(1)}, u32[]{:S(2)}, u32[]{:S(2)}) async-start(s32[16,1,16]{2,1,0:T(1,128)} %bitcast.9), calls=%async_computation.1 | async-start | bytes 16384 | tf_op jit(solution)/shard_map/all_to_all | solution.py:41
  45.1 111.4 %all-to-all-start.3 = ((bf16[16,16,128,128]{3,2,1,0:T(8,128)(2,1)}), bf16[16,16,128,128]{3,2,1,0:T(8,128)(2,1)}, u32[]{:S(2)}, u32[]{:S(2)}) async-start(bf16[16,16,128,128]{3,2,1,0:T(8,128)(2,1)} %bitcast.101), calls=%async_computation.3 | async-start | bytes 16777216 | tf_op jit(solution)/shard_map/all_to_all | solution.py:46
  156.5 143.5 %all-to-all-start.2 = ((bf16[16,16,128,128]{3,2,1,0:T(8,128)(2,1)}), bf16[16,16,128,128]{3,2,1,0:T(8,128)(2,1)}, u32[]{:S(2)}, u32[]{:S(2)}) async-start(bf16[16,16,128,128]{3,2,1,0:T(8,128)(2,1)} %bitcast.100), calls=%async_computation.2 | async-start | bytes 16777216 | tf_op jit(solution)/shard_map/all_to_all | solution.py:45
  205.9 127.9 %copy-start.1 = (s32[32,4]{0,1:T(4,128)S(1)}, s32[32,4]{0,1:T(4,128)}, u32[]{:S(2)}) copy-start(s32[32,4]{0,1:T(4,128)} %param.11) | copy-start | bytes 1540
  205.9 127.9 %copy-start.2 = (s32[32,4]{0,1:T(4,128)S(1)}, s32[32,4]{0,1:T(4,128)}, u32[]{:S(2)}) copy-start(s32[32,4]{0,1:T(4,128)} %param.10) | copy-start | bytes 1540
  300.0 79.0 %all-to-all-start = ((bf16[512,16,128]{2,0,1:T(8,128)(2,1)}), bf16[512,16,128]{2,0,1:T(8,128)(2,1)}, u32[]{:S(2)}, u32[]{:S(2)}) async-start(bf16[512,16,128]{2,0,1:T(8,128)(2,1)} %copy.59), calls=%async_computation | async-start | bytes 4194304 | tf_op jit(solution)/shard_map/all_to_all | solution.py:13
  371.0 5.1 %copy-start = (bf16[128,128,128]{2,1,0:T(8,128)(2,1)S(1)}, bf16[128,128,128]{2,1,0:T(8,128)(2,1)}, u32[]{:S(2)}) copy-start(bf16[128,128,128]{2,1,0:T(8,128)(2,1)} %gather_fusion.1) | copy-start | bytes 12582916
where the time goes:
time: 448 us; the launch traced here: 446 us
  waiting for transfers between devices  188 us (42%)
  local copies, waits for them, and re-layouts  83.5 us (19%)
  starting transfers between devices  66.5 us (15%)
  blocking collectives  52.6 us (12%)
  other arithmetic  28.8 us (6%)
  matrix products  26.2 us (6%)
    all_to_all x1, waiting for transfers between devices, on_device(): lax.all_to_all(picked_keys, 'seq', split_axis=0, concat_axis=0, tiled=True)  94.1 us
    all_to_all x1, waiting for transfers between devices, on_device(): lax.all_to_all(picked_values, 'seq', split_axis=0, concat_axis=0, tiled=T...  93.9 us
    all_to_all x1, starting transfers between devices, on_device(): lax.all_to_all(picked_keys, 'seq', split_axis=0, concat_axis=0, tiled=True)  45.9 us
    all_gather x1, blocking collectives, on_device(): lax.all_gather(key_mean, 'seq', axis=0, tiled=True)  28.6 us
    all_gather x1, blocking collectives, on_device(): lax.all_gather(value_mean, 'seq', axis=0, tiled=True)  24 us
    scatter x1, local copies, waits for them, and re-layouts, on_device(): jnp.zeros((seq_count, capacity), jnp.int32).at[owner_flat, slot_index]  17.8 us
    dot_general x8, matrix products, attend_group(): jnp.einsum('gthd,gud->gthu', query_part, keys_flat, preferred_element_typ...  12.4 us
    dynamic_slice x8, local copies, waits for them, and re-layouts, on_device(): attended = lax.map(attend_group, packed)  11.2 us
  transfers between devices with their start and end apart: 4, of which 2 were waited for; matrix products, arithmetic and copies ran while one was open for 10% of the time, Pallas kernels for 0%

commit v1 on v0

v1 whole, which is shorter than its diff:
```python
import functools
import math

import jax
import jax.numpy as jnp
from jax import lax
from jax.experimental import pallas as pl
from jax.experimental.pallas import tpu as pltpu
from jax.sharding import PartitionSpec as P

MESH = pl.DeviceIdType.MESH
BLK = 128
HD = 128
SIDE = 4
BLOCKS = 32
LISTED = 128
CAP = 64
HEADS = 8


def move_kernel(
    own, q_in, owner_r, local_r, owner_c, local_c,
    far, ownkv, means, q_out,
    row, sendbuf, recv, sel, tab_out, tab_in, tab_s, pos_v, pos_s, mrow, mall, nat,
    a_send, a_recv, t_send, t_recv, s_send, s_recv, m_send, m_recv,
    q_send, q_recv, x_send, x_recv, l_sem,
):
    seq, head = lax.axis_index("seq"), lax.axis_index("head")
    core = head % 2
    x, z = seq // SIDE, seq % SIDE
    a, b = x + core * (z - x), z + core * (x - z)
    stride_a, stride_b = SIDE - 3 * core, 1 + 3 * core
    sibling = head + 1 - 2 * core

    def on_a(k):
        return (a + k) % SIDE

    def on_b(k):
        return (b + k) % SIDE

    def dev_a(k):
        return (on_a(k) * stride_a + b * stride_b, head)

    def dev_b(k):
        return (a * stride_a + on_b(k) * stride_b, head)

    def remote(src, dst, send, recv_, dev):
        return pltpu.make_async_remote_copy(
            src_ref=src, dst_ref=dst, send_sem=send, recv_sem=recv_,
            device_id=dev, device_id_type=MESH,
        )

    barrier = pltpu.get_barrier_semaphore()
    peers = [dev_a(1), dev_a(3), dev_b(1), dev_b(2), dev_b(3)]
    peers += [(seq, (head + k) % HEADS) for k in range(1, HEADS)]
    for dev in peers:
        pl.semaphore_signal(barrier, inc=1, device_id=dev, device_id_type=MESH)
    pl.semaphore_wait(barrier, len(peers))

    half = BLOCKS // 2
    lo, hi = pl.ds(0, half), pl.ds(half, half)
    gather = [
        remote(own.at[lo], row.at[a, lo], a_send.at[0], a_recv.at[0], dev_a(1)),
        remote(own.at[hi], row.at[a, hi], a_send.at[2], a_recv.at[2], dev_a(3)),
        remote(own.at[hi], row.at[a, hi], a_send.at[1], a_recv.at[1], dev_a(1)),
        remote(own.at[lo], row.at[a, lo], a_send.at[3], a_recv.at[3], dev_a(3)),
    ]
    for copy in gather:
        copy.start()
    queries = [
        remote(
            q_in.at[(head + k) % HEADS], q_out.at[head], q_send.at[k - 1], q_recv.at[k - 1],
            (seq, (head + k) % HEADS),
        )
        for k in range(1, HEADS)
    ]
    for copy in queries:
        copy.start()
    own_row = pltpu.make_async_copy(own, row.at[a], l_sem.at[0])
    own_q = pltpu.make_async_copy(q_in.at[head], q_out.at[head], l_sem.at[1])
    own_out = pltpu.make_async_copy(own, ownkv.at[core], l_sem.at[2])
    own_x = remote(own, ownkv.at[core], x_send.at[0], x_recv.at[0], (seq, sibling))
    for copy in (own_row, own_q, own_out, own_x):
        copy.start()

    ow_r, ow_c = owner_r[...], owner_c[...]
    ar, br = ow_r // SIDE, ow_r % SIDE
    ac, bc = ow_c // SIDE, ow_c % SIDE
    ar, br = ar + core * (br - ar), br + core * (ar - br)
    ac, bc = ac + core * (bc - ac), bc + core * (ac - bc)
    lane = lax.broadcasted_iota(jnp.int32, (LISTED, LISTED), 1)
    sub = lax.broadcasted_iota(jnp.int32, (LISTED, LISTED), 0)
    same = bc == br
    rank_r = jnp.sum(jnp.where(same & (sub < lane), 1, 0), axis=0, keepdims=True)
    rank_c = jnp.sum(
        jnp.where(same & (lane < sub), 1.0, 0.0).astype(jnp.float32), axis=1, keepdims=True
    ).astype(jnp.int32)
    idx_c = ac * BLOCKS + local_c[...]
    place_c = bc * LISTED + rank_c
    for g in range(SIDE):
        table = jnp.sum(
            jnp.where(place_c == lane + g * LISTED, idx_c, 0), axis=0, keepdims=True
        )
        tab_out[g] = jnp.broadcast_to(table, (8, LISTED))
    pos_v[...] = jnp.broadcast_to(br * CAP + rank_r, (8, LISTED))
    tables = [
        remote(tab_out.at[on_b(k)], tab_in.at[k - 1], t_send.at[k - 1], t_recv.at[k - 1], dev_b(k))
        for k in range(1, SIDE)
    ]
    for copy in tables:
        copy.start()
    own_tab = pltpu.make_async_copy(tab_out.at[b], tab_s.at[0], l_sem.at[3])
    pos_copy = pltpu.make_async_copy(pos_v, pos_s, l_sem.at[4])
    own_tab.start()
    pos_copy.start()

    gather[0].wait_recv()
    pass_r = remote(row.at[on_a(3), lo], row.at[on_a(3), lo], a_send.at[4], a_recv.at[4], dev_a(1))
    pass_r.start()
    gather[1].wait_recv()
    pass_l = remote(row.at[on_a(1), hi], row.at[on_a(1), hi], a_send.at[5], a_recv.at[5], dev_a(3))
    pass_l.start()
    gather[2].wait_recv()
    gather[3].wait_recv()
    pass_r.wait_recv()
    pass_l.wait_recv()
    own_row.wait()

    tab_copies = []
    for k in range(1, SIDE):
        tables[k - 1].wait_recv()
        copy = pltpu.make_async_copy(tab_in.at[k - 1], tab_s.at[k], l_sem.at[4 + k])
        copy.start()
        tab_copies.append(copy)
    own_tab.wait()
    for copy in tab_copies:
        copy.wait()

    rows = row.reshape(SIDE * BLOCKS, BLK, HD)
    part = CAP // 2
    picks = []
    for n, k in enumerate((2, 1, 3)):
        for p in range(2):

            @pl.loop(0, part)
            def _(i, k=k, p=p):
                sendbuf[k - 1, p * part + i] = rows[tab_s[k, 0, p * part + i]]

            copy = remote(
                sendbuf.at[k - 1, pl.ds(p * part, part)], recv.at[b, pl.ds(p * part, part)],
                s_send.at[2 * n + p], s_recv.at[2 * n + p], dev_b(-k % SIDE),
            )
            copy.start()
            picks.append(copy)

    @pl.loop(0, CAP)
    def _(i):
        recv[b, i] = rows[tab_s[0, 0, i]]

    take = 16
    pick_r = lax.broadcasted_iota(jnp.int32, (take, take * BLK), 0)
    pick_c = lax.broadcasted_iota(jnp.int32, (take, take * BLK), 1) // BLK
    averager = jnp.where(pick_r == pick_c, 1.0 / BLK, 0.0).astype(jnp.bfloat16)

    @pl.loop(0, SIDE * BLOCKS // take)
    def _(i):
        start = pl.multiple_of(i * take, take)
        tokens = rows[pl.ds(start, take)].reshape(take * BLK, HD)
        mean = jnp.dot(averager, tokens, preferred_element_type=jnp.float32)
        mrow[pl.ds(start, take)] = mean.astype(jnp.bfloat16)

    mean_sends = [
        remote(mrow, mall.at[b], m_send.at[k - 1], m_recv.at[k - 1], dev_b(k))
        for k in range(1, SIDE)
    ]
    for copy in mean_sends:
        copy.start()
    mall[b] = mrow[...]
    for copy in mean_sends:
        copy.wait_recv()
    for bb in range(SIDE):
        for aa in range(SIDE):
            nat[aa * stride_a + bb * stride_b] = mall[bb, pl.ds(aa * BLOCKS, BLOCKS)]
    mean_x = remote(nat, means.at[core], x_send.at[1], x_recv.at[1], (seq, sibling))
    mean_out = pltpu.make_async_copy(nat, means.at[core], l_sem.at[8])
    mean_x.start()
    mean_out.start()

    for copy in picks:
        copy.wait_recv()
    pos_copy.wait()
    slots = recv.reshape(SIDE * CAP, BLK, HD)
    chunk = LISTED // 4
    outs = []
    for p in range(4):

        @pl.loop(0, chunk)
        def _(i, p=p):
            sel[p * chunk + i] = slots[pos_s[0, p * chunk + i]]

        where = pl.ds(p * chunk, chunk)
        to_x = remote(
            sel.at[where], far.at[core, where], x_send.at[2 + p], x_recv.at[2 + p], (seq, sibling)
        )
        to_out = pltpu.make_async_copy(sel.at[where], far.at[core, where], l_sem.at[9 + p])
        to_x.start()
        to_out.start()
        outs += [to_x, to_out]

    for copy in outs + [own_q, own_out, own_x, mean_x, mean_out]:
        copy.wait()
    for copy in queries:
        copy.wait()
    for copy in gather + [pass_r, pass_l] + tables + picks + mean_sends:
        copy.wait_send()


def move(own, q_in, owner, local):
    dma = pltpu.SemaphoreType.DMA
    bf16, i32 = jnp.bfloat16, jnp.int32
    vmem, hbm = pl.BlockSpec(memory_space=pltpu.VMEM), pl.BlockSpec(memory_space=pl.ANY)
    return pl.pallas_call(
        move_kernel,
        out_shape=(
            jax.ShapeDtypeStruct((2, LISTED, BLK, HD), bf16),
            jax.ShapeDtypeStruct((2, BLOCKS, BLK, HD), bf16),
            jax.ShapeDtypeStruct((2, SIDE * SIDE, BLOCKS, HD), bf16),
            jax.ShapeDtypeStruct(q_in.shape, bf16),
        ),
        in_specs=[vmem, hbm, vmem, vmem, vmem, vmem],
        out_specs=(hbm, hbm, hbm, hbm),
        scratch_shapes=[
            pltpu.VMEM((SIDE, BLOCKS, BLK, HD), bf16),
            pltpu.VMEM((SIDE - 1, CAP, BLK, HD), bf16),
            pltpu.VMEM((SIDE, CAP, BLK, HD), bf16),
            pltpu.VMEM((LISTED, BLK, HD), bf16),
            pltpu.VMEM((SIDE, 8, LISTED), i32),
            pltpu.VMEM((SIDE - 1, 8, LISTED), i32),
            pltpu.SMEM((SIDE, 8, LISTED), i32),
            pltpu.VMEM((8, LISTED), i32),
            pltpu.SMEM((8, LISTED), i32),
            pltpu.VMEM((SIDE * BLOCKS, HD), bf16),
            pltpu.VMEM((SIDE, SIDE * BLOCKS, HD), bf16),
            pltpu.VMEM((SIDE * SIDE, BLOCKS, HD), bf16),
            dma((6,)), dma((6,)), dma((3,)), dma((3,)), dma((6,)), dma((6,)), dma((3,)), dma((3,)),
            dma((HEADS - 1,)), dma((HEADS - 1,)), dma((6,)), dma((6,)), dma((13,)),
        ],
        compiler_params=pltpu.CompilerParams(
            collective_id=0, has_side_effects=True, vmem_limit_bytes=48 * 2**20
        ),
        cost_estimate=pl.CostEstimate(flops=0, bytes_accessed=32 * 2**20, transcendentals=0),
        name="move",
    )(
        own, q_in, owner.reshape(1, LISTED), local.reshape(1, LISTED),
        owner.reshape(LISTED, 1), local.reshape(LISTED, 1),
    )


def attend_kernel(ids, q_ref, ko_ref, vo_ref, kf_ref, vf_ref, km_ref, vm_ref, o_ref):
    block = pl.program_id(0)
    f32, bf16 = jnp.float32, jnp.bfloat16
    rows = 2 * BLK
    to_log2 = math.log2(math.e)
    scale = HD**-0.5 * to_log2
    q = q_ref[...].reshape(rows, HD)

    def scores(left, right):
        return lax.dot_general(left, right, (((1,), (1,)), ((), ())), preferred_element_type=f32)

    which = lax.broadcasted_iota(jnp.int32, (8, rows), 0)
    column = lax.broadcasted_iota(jnp.int32, (8, rows), 1)
    parity = jnp.where(which == column % 2, 1.0 / BLK, 0.0).astype(bf16)
    q_mean = jnp.dot(parity, q, preferred_element_type=f32)
    high = q_mean.astype(bf16)
    rest = q_mean - high.astype(f32)
    mid = rest.astype(bf16)
    low = (rest - mid.astype(f32)).astype(bf16)
    km = km_ref[0]
    coarse = (scores(high, km) + scores(mid, km) + scores(low, km)) * scale + math.log2(BLK)
    number = lax.broadcasted_iota(jnp.int32, coarse.shape, 1)
    gone = number == ids[block * 5]
    for r in range(1, 5):
        gone = gone | (number == ids[block * 5 + r])
    coarse = jnp.where(gone, -1e30, coarse)
    c_max = jnp.max(coarse, axis=1, keepdims=True)
    c_w = jnp.where(gone, 0.0, jnp.exp2(coarse - c_max))
    c_sum = jnp.sum(c_w, axis=1, keepdims=True)
    c_val = jnp.dot(c_w.astype(bf16), vm_ref[0], preferred_element_type=f32)

    odd = lax.broadcasted_iota(jnp.int32, (rows, 1), 0) % 2 == 1

    def per_row(stat):
        return jnp.where(odd, stat[1:2], stat[0:1])

    keys = [ko_ref[0, 0]] + [kf_ref[0, r] for r in range(4)]
    values = [vo_ref[0, 0]] + [vf_ref[0, r] for r in range(4)]
    fine = scores(q, jnp.concatenate(keys, axis=0)) * scale
    cm = per_row(c_max)
    top = jnp.maximum(cm, jnp.max(fine, axis=1, keepdims=True))
    weights = jnp.exp2(fine - top)
    alpha = jnp.exp2(cm - top)
    total = alpha * per_row(c_sum) + jnp.sum(weights, axis=1, keepdims=True)
    out = jnp.dot(
        weights.astype(bf16), jnp.concatenate(values, axis=0), preferred_element_type=f32
    )
    out = (out + alpha * per_row(c_val)) / total
    o_ref[...] = out.astype(bf16).reshape(BLK, 2, HD)


def attend(ids, q, ownkv, far, means):
    per = 512 // BLK
    one = (1, 1, BLK, HD)
    four = (1, 4, BLK, HD)
    whole = (1, means.shape[1], HD)
    return pl.pallas_call(
        attend_kernel,
        out_shape=jax.ShapeDtypeStruct((BLOCKS * BLK, 2, HD), jnp.bfloat16),
        grid_spec=pltpu.PrefetchScalarGridSpec(
            num_scalar_prefetch=1,
            grid=(BLOCKS,),
            in_specs=[
                pl.BlockSpec((1, BLK, 2, HD), lambda i, ids: (i // per, i % per, 0, 0)),
                pl.BlockSpec(one, lambda i, ids: (0, i, 0, 0)),
                pl.BlockSpec(one, lambda i, ids: (1, i, 0, 0)),
                pl.BlockSpec(four, lambda i, ids: (0, i, 0, 0)),
                pl.BlockSpec(four, lambda i, ids: (1, i, 0, 0)),
                pl.BlockSpec(whole, lambda i, ids: (0, 0, 0)),
                pl.BlockSpec(whole, lambda i, ids: (1, 0, 0)),
            ],
            out_specs=pl.BlockSpec((BLK, 2, HD), lambda i, ids: (i, 0, 0)),
        ),
        compiler_params=pltpu.CompilerParams(vmem_limit_bytes=32 * 2**20),
        name="attend",
    )(ids, q, ownkv, ownkv, far, far, means, means)


def on_device(queries, keys, values, refine_owner, refine_local):
    head = lax.axis_index("head")
    kv = head // 2
    q_in = queries.reshape(512, HEADS, 2, HD).transpose(1, 0, 2, 3)
    own = lax.cond(
        head % 2 == 0,
        lambda: lax.dynamic_index_in_dim(keys, kv, 1, keepdims=False),
        lambda: lax.dynamic_index_in_dim(values, kv, 1, keepdims=False),
    ).reshape(BLOCKS, BLK, HD)
    far, ownkv, means, q = move(own, q_in, refine_owner, refine_local)
    first = lax.axis_index("seq") * BLOCKS
    own_ids = (first + jnp.arange(BLOCKS, dtype=jnp.int32))[:, None]
    ids = jnp.concatenate([own_ids, refine_owner * BLOCKS + refine_local], axis=1).reshape(-1)
    return attend(ids, q, ownkv, far, means.reshape(2, -1, HD))


def solution(mesh):
    return jax.shard_map(
        on_device,
        mesh=mesh,
        in_specs=(
            P(("seq", "head"), None, None),
            P("seq", None, None),
            P("seq", None, None),
            P("seq", None),
            P("seq", None),
        ),
        out_specs=P("seq", "head", None),
        check_vma=False,
    )
```

time: 448 us -> 145 us (0.32)
  the two profiles are of different devices: /device:TPU:10 before, /device:TPU:1 now
where the time goes in v1:
time: 145 us
  Pallas kernels  126 us (87%)
  local copies, waits for them, and re-layouts  18.2 us (13%)
    pallas_call x1, Pallas kernels, move(): pl.pallas_call(move_kernel, out_shape=(jax.ShapeDtypeStruct((2, LISTED, B...  91.3 us
    pallas_call x1, Pallas kernels, attend(): pl.pallas_call(attend_kernel, out_shape=jax.ShapeDtypeStruct((BLOCKS * BL...  35 us
    unnamed x15, local copies, waits for them, and re-layouts  11.8 us
    reshape x1, local copies, waits for them, and re-layouts, on_device(): q_in = queries.reshape(512, HEADS, 2, HD).transpose(1, 0, 2, 3)  2.94 us

profile of v1, /device:TPU:1, one launch (start us, length us, event | category | flops | bytes accessed | tf_op | source)
XLA Modules:
  0.0 144.6 jit_solution(3756133600928924845)
XLA Ops:
  0.0 5.3 %copy.37 = bf16[4096,4,128]{2,1,0:T(4,128)(2,1)} copy(bf16[4096,4,128]{2,1,0:T(4,128)(2,1)} %param.9) | data formatting | bytes 8388608
  5.3 0.0 copy-start.5
  5.3 0.0 copy-start.4
  5.3 0.0 copy-start.3
  5.3 2.9 %copy.15 = bf16[4096,4,128]{2,0,1:T(8,128)(2,1)S(1)} copy(bf16[4096,4,128]{2,1,0:T(4,128)(2,1)} %get-tuple-element.40) | data formatting | bytes 8388608 | tf_op jit(solution)/shard_map/cond | solution.py:341
  8.2 0.1 constant_dynamic-slice_fusion
  8.3 0.0 copy-done.5
  8.3 0.1 copy.18
  8.4 0.1 reshape.40.owner_c
  8.5 0.0 copy-done.4
  8.5 0.1 copy.19
  8.5 0.1 reshape.41.local_c
  8.6 0.1 reshape.35.owner_r
  8.7 0.1 reshape.36.local_r
  8.8 0.0 copy-done.3
  8.9 2.9 %copy.27 = bf16[512,8,2,128]{3,2,0,1:T(2,128)(2,1)} copy(bf16[512,8,2,128]{3,2,1,0:T(2,128)(2,1)S(1)} %bitcast.10) | data formatting | bytes 4194304 | tf_op jit(solution)/shard_map/reshape | solution.py:340
  11.8 91.3 %move.1 = (bf16[2,128,128,128]{3,2,1,0:T(8,128)(2,1)}, bf16[2,32,128,128]{3,2,1,0:T(8,128)(2,1)S(1)}, bf16[2,16,32,128]{3,2,1,0:T(8,128)(2,1)S(1)}, bf16[8,512,2,128]{3,2,1,0:T(2,128)(2,1)S(1)}) custom-call(bf16[32,128,128]{2,1,0:T(8,128)(2,1)S(1)} %bitcast.6, bf16[8,512,2,128]{3,2,1,0:T(2,128)(2,1)} %bitcast.9, s32[1,128]{1,0:T(1,128)S(1)} %reshape.35.owner_r, ...), custom_call_target="tpu_custom_call" | custom-call | bytes 33554432 | tf_op jit(solution)/shard_map/move/pallas_call | solution.py:222
  103.1 0.0 copy-start.1
  103.1 1.3 copy-done.1
  104.4 0.1 copy.14
  104.5 0.1 reshape.32.ids
  104.6 0.0 copy-start
  104.6 3.4 %copy-done = bf16[2,128,128,128]{3,2,1,0:T(8,128)(2,1)S(1)} copy-done((bf16[2,128,128,128]{3,2,1,0:T(8,128)(2,1)S(1)}, bf16[2,128,128,128]{3,2,1,0:T(8,128)(2,1)}, u32[]{:S(2)}) %copy-start) | copy-done | bytes 8388632
  108.0 0.0 copy-start.2
  108.0 1.6 %copy-done.2 = bf16[8,512,2,128]{3,2,1,0:T(2,128)(2,1)S(1)} copy-done((bf16[8,512,2,128]{3,2,1,0:T(2,128)(2,1)S(1)}, bf16[8,512,2,128]{3,2,1,0:T(2,128)(2,1)}, u32[]{:S(2)}) %copy-start.2) | copy-done | bytes 2097176
  109.6 35.0 %attend.1 = bf16[4096,2,128]{2,1,0:T(2,128)(2,1)} custom-call(s32[160]{0:T(256)S(1)} %reshape.32.ids, bf16[8,512,2,128]{3,2,1,0:T(2,128)(2,1)S(1)} %copy-done.2, bf16[2,32,128,128]{3,2,1,0:T(8,128)(2,1)S(1)} %get-tuple-element.44.ko_ref.vo_ref, bf16[2,32,128,128]{3,2,1,0:T(8,128)(2,1)S(1)} %get-tuple-element.44.ko_ref.vo_ref, ...), custom_call_target="tpu_custom_call" | custom-call | tf_op jit(solution)/shard_map/attend/pallas_call | solution.py:315
  (4 shorter events, 0.0 us)
Async XLA Ops:
  5.3 3.0 %copy-start.5 = (s32[32,4]{0,1:T(4,128)S(1)}, s32[32,4]{0,1:T(4,128)}, u32[]{:S(2)}) copy-start(s32[32,4]{0,1:T(4,128)} %param.10) | copy-start | bytes 1540
  5.3 3.2 %copy-start.4 = (s32[32,4]{0,1:T(4,128)S(1)}, s32[32,4]{0,1:T(4,128)}, u32[]{:S(2)}) copy-start(s32[32,4]{0,1:T(4,128)} %param.11) | copy-start | bytes 1540
  5.3 3.5 %copy-start.3 = (bf16[512,16,128]{2,1,0:T(8,128)(2,1)S(1)}, bf16[512,16,128]{2,1,0:T(8,128)(2,1)}, u32[]{:S(2)}) copy-start(bf16[512,16,128]{2,1,0:T(8,128)(2,1)} %param.7) | copy-start | bytes 6291460
  103.1 1.3 copy-start.1
  104.6 3.4 %copy-start = (bf16[2,128,128,128]{3,2,1,0:T(8,128)(2,1)S(1)}, bf16[2,128,128,128]{3,2,1,0:T(8,128)(2,1)}, u32[]{:S(2)}) copy-start(bf16[2,128,128,128]{3,2,1,0:T(8,128)(2,1)} %get-tuple-element.45.kf_ref.vf_ref) | copy-start | bytes 25165828
  108.0 1.6 %copy-start.2 = (bf16[8,512,2,128]{3,2,1,0:T(2,128)(2,1)S(1)}, bf16[8,512,2,128]{3,2,1,0:T(2,128)(2,1)}, u32[]{:S(2)}) copy-start(bf16[8,512,2,128]{3,2,1,0:T(2,128)(2,1)} %copy-done.1) | copy-start | bytes 6291460

commit v2 on v0

v2 whole, which is shorter than its diff:
```python
import functools
import math

import jax
import jax.numpy as jnp
from jax import lax
from jax.experimental import pallas as pl
from jax.experimental.pallas import tpu as pltpu
from jax.sharding import PartitionSpec as P

MESH = pl.DeviceIdType.MESH
BLK = 128
HD = 128
KVH = 4
SIDE = 4
BLOCKS = 32
LISTED = 128
REFINE = 4
HEADS = 8
HALF = BLK // 2
ROWS = 2 * BLK
MIB = 2**20
F32, BF16, I32 = jnp.float32, jnp.bfloat16, jnp.int32
DMA = pltpu.SemaphoreType.DMA


class Place:
    def __init__(self):
        self.seq, self.head = lax.axis_index("seq"), lax.axis_index("head")
        self.core = self.head % 2
        x, z = self.seq // SIDE, self.seq % SIDE
        self.a, self.b = x + self.core * (z - x), z + self.core * (x - z)
        self.stride_a, self.stride_b = SIDE - 3 * self.core, 1 + 3 * self.core
        self.sibling = (self.seq, self.head + 1 - 2 * self.core)

    def on_a(self, k):
        return (self.a + k) % SIDE

    def on_b(self, k):
        return (self.b + k) % SIDE

    def dev_a(self, k):
        return (self.on_a(k) * self.stride_a + self.b * self.stride_b, self.head)

    def dev_b(self, k):
        return (self.a * self.stride_a + self.on_b(k) * self.stride_b, self.head)

    def dev_head(self, k):
        return (self.seq, (self.head + k) % HEADS)


def remote(src, dst, send, recv, dev):
    return pltpu.make_async_remote_copy(
        src_ref=src, dst_ref=dst, send_sem=send, recv_sem=recv, device_id=dev, device_id_type=MESH
    )


def greet(peers):
    barrier = pltpu.get_barrier_semaphore()
    for dev in peers:
        pl.semaphore_signal(barrier, inc=1, device_id=dev, device_id_type=MESH)
    pl.semaphore_wait(barrier, len(peers))


def start(copies):
    for copy in copies:
        copy.start()


def spread_kernel(
    keys, values, queries, owner_r, local_r, owner_c, local_c,
    rows, own, means, q_out, tabs, pos,
    kv_in, q_in, half, row, both, q_st, tab_out, tab_in, pos_v, mean_a, mean_b,
    in_sem, a_send, a_recv, q_send, q_recv, t_send, t_recv, m_send, m_recv, x_send, x_recv, l_sem,
):
    at = Place()
    kv = at.head // 2
    parts = 2
    per = BLOCKS // parts
    loads = []
    for t, src in enumerate((keys, values)):
        for p in range(parts):
            where = pl.ds(p * per, per)
            loads.append(
                pltpu.make_async_copy(
                    src.at[where, pl.ds(at.core * (HALF * KVH), HALF * KVH)],
                    kv_in.at[t, where],
                    in_sem.at[t * parts + p],
                )
            )
    loads.append(pltpu.make_async_copy(queries, q_in, in_sem.at[2 * parts]))
    start(loads)

    greet(
        [at.dev_a(k) for k in range(1, SIDE)]
        + [at.dev_b(k) for k in range(1, SIDE)]
        + [at.dev_head(k) for k in range(1, HEADS)]
    )

    out_row = lax.broadcasted_iota(I32, (HALF, HALF * KVH), 0)
    in_row = lax.broadcasted_iota(I32, (HALF, HALF * KVH), 1)
    chooser = jnp.where(in_row == out_row * KVH + kv, 1.0, 0.0).astype(BF16)
    my_half = pl.ds(at.core * HALF, HALF)
    gather, to_x = [], []
    for t in range(2):
        for p in range(parts):
            loads[t * parts + p].wait()

            @pl.loop(p * per // 4, (p + 1) * per // 4)
            def _(i, t=t):
                for u in range(4):
                    picked = jnp.dot(chooser, kv_in[t, i * 4 + u], preferred_element_type=F32)
                    picked = picked.astype(BF16)
                    half[t, i * 4 + u] = picked
                    both[t, i * 4 + u, my_half] = picked

            if p == 1:
                order = ((0, 1, 0), (1, 3, 2), (1, 1, 1), (0, 3, 3))
                for part, k, n in order:
                    where = pl.ds(part * per, per)
                    gather.append(
                        remote(
                            half.at[t, where], row.at[t, at.a, where],
                            a_send.at[t, n], a_recv.at[t, n], at.dev_a(k),
                        )
                    )
                start(gather[-4:])
        to_x.append(
            remote(
                both.at[t, :, my_half], both.at[t, :, my_half],
                x_send.at[t], x_recv.at[t], at.sibling,
            )
        )
        to_x[-1].start()
    own_row = [pltpu.make_async_copy(half.at[t], row.at[t, at.a], l_sem.at[t]) for t in range(2)]
    start(own_row)

    loads[-1].wait()
    step = 16
    out_row = lax.broadcasted_iota(I32, (16 * step, 16 * step), 0)
    in_row = lax.broadcasted_iota(I32, (16 * step, 16 * step), 1)
    pair, rest = out_row // (2 * step), out_row % (2 * step)
    order = jnp.where(in_row == (rest // 2) * 16 + pair * 2 + rest % 2, 1.0, 0.0).astype(BF16)
    chunks = q_in.shape[0] // (16 * step)

    @pl.loop(0, chunks // 2)
    def _(i):
        for u in range(2):
            first = pl.multiple_of((i * 2 + u) * 16 * step, 16 * step)
            turned = jnp.dot(order, q_in[pl.ds(first, 16 * step)], preferred_element_type=F32)
            turned = turned.astype(BF16)
            place = pl.multiple_of((i * 2 + u) * 2 * step, 2 * step)
            for h in range(HEADS):
                q_st[h, pl.ds(place, 2 * step)] = turned[h * 2 * step : (h + 1) * 2 * step]

    asked = [
        remote(
            q_st.at[(at.head + k) % HEADS], q_out.at[at.head],
            q_send.at[k - 1], q_recv.at[k - 1], at.dev_head(k),
        )
        for k in range(1, HEADS)
    ]
    start(asked)
    own_q = pltpu.make_async_copy(q_st.at[at.head], q_out.at[at.head], l_sem.at[2])
    own_q.start()

    ow_r, ow_c = owner_r[...], owner_c[...]
    ar, br = ow_r // SIDE, ow_r % SIDE
    ac, bc = ow_c // SIDE, ow_c % SIDE
    br, bc = br + at.core * (ar - br), bc + at.core * (ac - bc)
    ac = ac + at.core * (ow_c % SIDE - ac)
    id_r, id_c = ow_r * BLOCKS + local_r[...], ow_c * BLOCKS + local_c[...]
    lane = lax.broadcasted_iota(I32, (LISTED, LISTED), 1)
    sub = lax.broadcasted_iota(I32, (LISTED, LISTED), 0)
    twin = id_r == id_c

    def count(mask, axis):
        ones = jnp.where(mask, 1.0, 0.0).astype(F32)
        return jnp.sum(ones, axis=axis, keepdims=True).astype(I32)

    first_r = count(twin & (sub < lane), 0) == 0
    first_c = count(twin & (lane < sub), 1) == 0
    rank_c = count((bc == br) & (lane < sub) & first_r, 1)
    pos_r = jnp.sum(jnp.where(twin & first_c, rank_c, 0), axis=0, keepdims=True)
    idx_c = ac * BLOCKS + local_c[...]
    for g in range(SIDE):
        wanted = first_c & (bc == g) & (rank_c == lane)
        table = jnp.sum(jnp.where(wanted, idx_c, 0), axis=0, keepdims=True)
        tab_out[g] = jnp.broadcast_to(table, (8, LISTED))
    pos_v[...] = jnp.broadcast_to(br * LISTED + pos_r, (8, LISTED))
    tables = [
        remote(
            tab_out.at[at.on_b(k)], tab_in.at[k], t_send.at[k - 1], t_recv.at[k - 1], at.dev_b(k)
        )
        for k in range(1, SIDE)
    ]
    start(tables)
    tab_in[0] = tab_out[at.b]
    pos_copy = pltpu.make_async_copy(pos_v, pos, l_sem.at[3])
    pos_copy.start()

    passed = []
    lower, upper = pl.ds(0, per), pl.ds(per, per)
    for t in range(2):
        gather[4 * t].wait_recv()
        ref = row.at[t, at.on_a(3), lower]
        passed.append(remote(ref, ref, a_send.at[t, 4], a_recv.at[t, 4], at.dev_a(1)))
        passed[-1].start()
        gather[4 * t + 1].wait_recv()
        ref = row.at[t, at.on_a(1), upper]
        passed.append(remote(ref, ref, a_send.at[t, 5], a_recv.at[t, 5], at.dev_a(3)))
        passed[-1].start()

    take = 16
    pick_r = lax.broadcasted_iota(I32, (take, take * BLK), 0)
    pick_c = lax.broadcasted_iota(I32, (take, take * BLK), 1) // BLK
    averager = jnp.where(pick_r == pick_c, 1.0 / BLK, 0.0).astype(BF16)
    for t in range(2):
        to_x[t].wait_recv()
    for t in range(2):
        for i in range(BLOCKS // take):
            where = pl.ds(i * take, take)
            tokens = both[t, where].reshape(take * BLK, HD)
            mean = jnp.dot(averager, tokens, preferred_element_type=F32)
            mean_a[at.a, t, where] = mean.astype(BF16)
    own_out = pltpu.make_async_copy(both, own, l_sem.at[4])
    own_out.start()
    along_a = [
        remote(
            mean_a.at[at.a], mean_a.at[at.a], m_send.at[k - 1], m_recv.at[k - 1], at.dev_a(k)
        )
        for k in range(1, SIDE)
    ]
    start(along_a)
    for copy in along_a:
        copy.wait_recv()
    for k in range(SIDE):
        mean_b[at.b, k] = mean_a[k]
    along_b = [
        remote(
            mean_b.at[at.b], mean_b.at[at.b], m_send.at[k + 2], m_recv.at[k + 2], at.dev_b(k)
        )
        for k in range(1, SIDE)
    ]
    start(along_b)
    for copy in along_b:
        copy.wait_recv()
    mean_out = [
        pltpu.make_async_copy(
            mean_b.at[n, m], means.at[m * at.stride_a + n * at.stride_b], l_sem.at[7 + n * SIDE + m]
        )
        for n in range(SIDE)
        for m in range(SIDE)
    ]
    start(mean_out)
    for copy in tables:
        copy.wait_recv()
    tab_copy = pltpu.make_async_copy(tab_in, tabs, l_sem.at[23])
    tab_copy.start()

    rows_out = []
    for t in range(2):
        gather[4 * t + 2].wait_recv()
        gather[4 * t + 3].wait_recv()
        passed[2 * t].wait_recv()
        passed[2 * t + 1].wait_recv()
        own_row[t].wait()
        rows_out.append(pltpu.make_async_copy(row.at[t], rows.at[t], l_sem.at[5 + t]))
        rows_out[-1].start()
    for copy in asked:
        copy.wait()
    for copy in rows_out + mean_out + [own_q, pos_copy, own_out, tab_copy]:
        copy.wait()
    for copy in gather + passed + to_x + tables + along_a + along_b:
        copy.wait_send()


def spread(keys, values, queries, owner, local):
    vmem, hbm = pl.BlockSpec(memory_space=pltpu.VMEM), pl.BlockSpec(memory_space=pl.ANY)
    q_rows = queries.shape[0] // HEADS
    row_shape = (2, SIDE, BLOCKS, HALF, HD)
    own_shape = (2, BLOCKS, BLK, HD)
    mean_shape = (2, BLOCKS, HD)
    return pl.pallas_call(
        spread_kernel,
        out_shape=(
            jax.ShapeDtypeStruct(row_shape, BF16),
            jax.ShapeDtypeStruct(own_shape, BF16),
            jax.ShapeDtypeStruct((SIDE * SIDE,) + mean_shape, BF16),
            jax.ShapeDtypeStruct((HEADS, q_rows, HD), BF16),
            jax.ShapeDtypeStruct((SIDE, 8, LISTED), I32),
            jax.ShapeDtypeStruct((8, LISTED), I32),
        ),
        in_specs=[hbm, hbm, hbm, vmem, vmem, vmem, vmem],
        out_specs=(hbm,) * 6,
        scratch_shapes=[
            pltpu.VMEM((2, BLOCKS, HALF * KVH, HD), BF16),
            pltpu.VMEM(queries.shape, BF16),
            pltpu.VMEM((2, BLOCKS, HALF, HD), BF16),
            pltpu.VMEM(row_shape, BF16),
            pltpu.VMEM(own_shape, BF16),
            pltpu.VMEM((HEADS, q_rows, HD), BF16),
            pltpu.VMEM((SIDE, 8, LISTED), I32),
            pltpu.VMEM((SIDE, 8, LISTED), I32),
            pltpu.VMEM((8, LISTED), I32),
            pltpu.VMEM((SIDE,) + mean_shape, BF16),
            pltpu.VMEM((SIDE, SIDE) + mean_shape, BF16),
            DMA((5,)), DMA((2, 6)), DMA((2, 6)), DMA((HEADS - 1,)), DMA((HEADS - 1,)),
            DMA((3,)), DMA((3,)), DMA((6,)), DMA((6,)), DMA((2,)), DMA((2,)), DMA((24,)),
        ],
        compiler_params=pltpu.CompilerParams(
            collective_id=0, has_side_effects=True, vmem_limit_bytes=60 * MIB
        ),
        name="spread",
    )(
        keys, values, queries, owner.reshape(1, LISTED), local.reshape(1, LISTED),
        owner.reshape(LISTED, 1), local.reshape(LISTED, 1),
    )


def scores(left, right):
    return lax.dot_general(left, right, (((1,), (1,)), ((), ())), preferred_element_type=F32)


def pick_kernel(
    cap, tabs, pos, ids, rows, own, means, q_hbm, out,
    row_k, row_v, both, mean, q, sendbuf, recv_k, recv_v, far, weights, base, q_mean, c_max, c_sum, c_val, o_st,
    in_sem, s_send, s_recv, x_send, x_recv, o_sem,
):
    at = Place()
    row, recv = (row_k, row_v), (recv_k, recv_v)
    loads = [pltpu.make_async_copy(rows.at[t], row[t], in_sem.at[t]) for t in range(2)]
    loads += [
        pltpu.make_async_copy(q_hbm, q, in_sem.at[2]),
        pltpu.make_async_copy(means, mean, in_sem.at[3]),
        pltpu.make_async_copy(own, both, in_sem.at[4]),
    ]
    start(loads)
    greet([at.dev_b(k) for k in range(1, SIDE)] + [at.sibling])

    picks = [[], []]
    offsets = (2, 1, 3)

    def collect(t):
        blocks = row[t].reshape(SIDE * BLOCKS, HALF, HD)
        loads[t].wait()
        for n, k in enumerate(offsets):

            @pl.loop(0, cap // 8)
            def _(i, k=k):
                for u in range(8):
                    sendbuf[t, k - 1, i * 8 + u] = blocks[tabs[k, 0, i * 8 + u]]

            picks[t].append(
                remote(
                    sendbuf.at[t, k - 1], recv[t].at[at.b],
                    s_send.at[t, n], s_recv.at[t, n], at.dev_b(-k % SIDE),
                )
            )
            if t == 0:
                picks[t][-1].start()

        @pl.loop(0, cap // 8)
        def _(i):
            for u in range(8):
                recv[t][at.b, i * 8 + u] = blocks[tabs[0, 0, i * 8 + u]]

    collect(0)
    collect(1)

    to_log2 = math.log2(math.e)
    scale = HD**-0.5 * to_log2
    which = lax.broadcasted_iota(I32, (8, ROWS), 0)
    column = lax.broadcasted_iota(I32, (8, ROWS), 1)
    parity = jnp.where(which == column % 2, 1.0 / BLK, 0.0).astype(BF16)
    loads[2].wait()
    loads[3].wait()
    per_owner = q.shape[1] // ROWS

    def q_rows(i):
        first = pl.multiple_of((i % per_owner) * ROWS, ROWS)
        return q[i // per_owner, pl.ds(first, ROWS)]

    @pl.loop(0, BLOCKS // 4)
    def _(i):
        for u in range(4):
            q_mean[i * 4 + u] = jnp.dot(parity, q_rows(i * 4 + u), preferred_element_type=F32)

    group = 8
    total_blocks = SIDE * SIDE * BLOCKS
    key_means = mean[:, 0].reshape(total_blocks, HD)
    value_means = mean[:, 1].reshape(total_blocks, HD)

    @pl.loop(0, BLOCKS // group)
    def _(i):
        where = pl.ds(i * group, group)
        means_f = q_mean[where].reshape(group * 8, HD)
        high = means_f.astype(BF16)
        rest = means_f - high.astype(F32)
        mid = rest.astype(BF16)
        low = (rest - mid.astype(F32)).astype(BF16)
        coarse = scores(high, key_means) + scores(mid, key_means) + scores(low, key_means)
        coarse = coarse * scale + math.log2(BLK)
        number = lax.broadcasted_iota(I32, coarse.shape, 1)
        listed = ids[pl.ds(pl.multiple_of(i * group * 8, group * 8), group * 8)]
        gone = number == listed[:, 0:1]
        for r in range(1, REFINE + 1):
            gone = gone | (number == listed[:, r : r + 1])
        coarse = jnp.where(gone, -1e30, coarse)
        top = jnp.max(coarse, axis=1, keepdims=True)
        part = jnp.where(gone, 0.0, jnp.exp2(coarse - top))
        c_max[where] = jnp.broadcast_to(top, (group * 8, HD)).reshape(group, 8, HD)
        total = jnp.sum(part, axis=1, keepdims=True)
        c_sum[where] = jnp.broadcast_to(total, (group * 8, HD)).reshape(group, 8, HD)
        value = jnp.dot(part.astype(BF16), value_means, preferred_element_type=F32)
        c_val[where] = value.reshape(group, 8, HD)

    for copy in picks[0]:
        copy.wait_send()
    start(picks[1])
    loads[4].wait()

    my_half = pl.ds(at.core * HALF, HALF)
    pieces = 4
    piece = LISTED // pieces

    def listed_blocks(t):
        for copy in picks[t]:
            copy.wait_recv()
        copies = []
        for p in range(pieces):

            @pl.loop(0, piece // 8)
            def _(i, p=p):
                for u in range(8):
                    e = p * piece + i * 8 + u
                    place = pos[0, e]
                    far[t, e, my_half] = recv[t][place // LISTED, place % LISTED]

            ref = far.at[t, pl.ds(p * piece, piece), my_half]
            copies.append(
                remote(ref, ref, x_send.at[t, p], x_recv.at[t, p], at.sibling)
            )
            copies[-1].start()
        return copies

    odd = lax.broadcasted_iota(I32, (ROWS, 1), 0) % 2 == 1

    def per_row(ref, i, width):
        return jnp.where(odd, ref[i, 1:2, :width], ref[i, 0:1, :width])

    key_copies = listed_blocks(0)
    blocks_piece = BLOCKS // pieces
    for p in range(pieces):
        key_copies[p].wait_recv()

        @pl.loop(p * blocks_piece // 2, (p + 1) * blocks_piece // 2)
        def _(j):
            for u in range(2):
                i = j * 2 + u
                block_keys = jnp.concatenate(
                    [both[0, i], far[0, pl.ds(i * REFINE, REFINE)].reshape(REFINE * BLK, HD)], axis=0
                )
                fine = scores(q_rows(i), block_keys) * scale
                coarse_top = per_row(c_max, i, 1)
                top = jnp.maximum(coarse_top, jnp.max(fine, axis=1, keepdims=True))
                fine = jnp.exp2(fine - top)
                alpha = jnp.exp2(coarse_top - top)
                total = alpha * per_row(c_sum, i, 1) + jnp.sum(fine, axis=1, keepdims=True)
                share = 1.0 / total
                weights[i] = (fine * share).astype(BF16)
                base[i] = (alpha * share) * per_row(c_val, i, HD)

    value_copies = listed_blocks(1)
    outs = []
    for p in range(pieces):
        value_copies[p].wait_recv()

        @pl.loop(p * blocks_piece // 2, (p + 1) * blocks_piece // 2)
        def _(j):
            for u in range(2):
                i = j * 2 + u
                block_values = jnp.concatenate(
                    [both[1, i], far[1, pl.ds(i * REFINE, REFINE)].reshape(REFINE * BLK, HD)], axis=0
                )
                result = jnp.dot(weights[i], block_values, preferred_element_type=F32) + base[i]
                o_st[i] = result.astype(BF16)

        where = pl.ds(p * blocks_piece, blocks_piece)
        outs.append(pltpu.make_async_copy(o_st.at[where], out.at[where], o_sem.at[p]))
        outs[-1].start()

    for copy in outs:
        copy.wait()
    for copy in key_copies + value_copies + picks[1]:
        copy.wait_send()


def pick(cap, collective_id, rows, own, means, q, tabs, pos, ids):
    smem, vmem = pl.BlockSpec(memory_space=pltpu.SMEM), pl.BlockSpec(memory_space=pltpu.VMEM)
    hbm = pl.BlockSpec(memory_space=pl.ANY)
    return pl.pallas_call(
        functools.partial(pick_kernel, cap),
        out_shape=jax.ShapeDtypeStruct((BLOCKS, ROWS, HD), BF16),
        in_specs=[smem, smem, vmem, hbm, hbm, hbm, hbm],
        out_specs=hbm,
        scratch_shapes=[
            pltpu.VMEM(rows.shape[1:], BF16),
            pltpu.VMEM(rows.shape[1:], BF16),
            pltpu.VMEM(own.shape, BF16),
            pltpu.VMEM(means.shape, BF16),
            pltpu.VMEM(q.shape, BF16),
            pltpu.VMEM((2, SIDE - 1, cap, HALF, HD), BF16),
            pltpu.VMEM((SIDE, cap, HALF, HD), BF16),
            pltpu.VMEM((SIDE, cap, HALF, HD), BF16),
            pltpu.VMEM((2, LISTED, BLK, HD), BF16),
            pltpu.VMEM((BLOCKS, ROWS, (REFINE + 1) * BLK), BF16),
            pltpu.VMEM((BLOCKS, ROWS, HD), F32),
            pltpu.VMEM((BLOCKS, 8, HD), F32),
            pltpu.VMEM((BLOCKS, 8, HD), F32),
            pltpu.VMEM((BLOCKS, 8, HD), F32),
            pltpu.VMEM((BLOCKS, 8, HD), F32),
            pltpu.VMEM((BLOCKS, ROWS, HD), BF16),
            DMA((5,)), DMA((2, 3)), DMA((2, 3)), DMA((2, 4)), DMA((2, 4)), DMA((4,)),
        ],
        compiler_params=pltpu.CompilerParams(
            collective_id=collective_id, has_side_effects=True, vmem_limit_bytes=60 * MIB
        ),
        name="pick",
    )(tabs, pos, ids, rows, own, means, q)


def on_device(queries, keys, values, refine_owner, refine_local):
    first = lax.axis_index("seq") * BLOCKS
    own_ids = (first + jnp.arange(BLOCKS, dtype=I32))[:, None]
    ids = jnp.concatenate([own_ids, refine_owner * BLOCKS + refine_local], axis=1)
    ids = jnp.repeat(ids, 8, axis=0)
    rows, own, means, q, tabs, pos = spread(
        keys.reshape(BLOCKS, BLK * KVH, HD),
        values.reshape(BLOCKS, BLK * KVH, HD),
        queries.reshape(-1, HD),
        refine_owner,
        refine_local,
    )
    out = pick(64, 1, rows, own, means, q, tabs, pos, ids)
    return out.reshape(BLOCKS * BLK, 2, HD)


def solution(mesh):
    return jax.shard_map(
        on_device,
        mesh=mesh,
        in_specs=(
            P(("seq", "head"), None, None),
            P("seq", None, None),
            P("seq", None, None),
            P("seq", None),
            P("seq", None),
        ),
        out_specs=P("seq", "head", None),
        check_vma=False,
    )
```

time: 448 us -> 110 us (0.25)
  the two profiles are of different devices: /device:TPU:10 before, /device:TPU:1 now
where the time goes in v2:
time: 110 us
  Pallas kernels  99.7 us (91%)
  local copies, waits for them, and re-layouts  9.47 us (9%)
    pallas_call x1, Pallas kernels, pick(): pl.pallas_call(functools.partial(pick_kernel, cap), out_shape=jax.ShapeDt...  60.3 us
    pallas_call x1, Pallas kernels, spread(): pl.pallas_call(spread_kernel, out_shape=(jax.ShapeDtypeStruct(row_shape,...  39.4 us
    unnamed x3, local copies, waits for them, and re-layouts  5.96 us

profile of v2, /device:TPU:1, one launch (start us, length us, event | category | flops | bytes accessed | tf_op | source)
XLA Modules:
  0.0 109.9 jit_solution(7261194380050740756)
XLA Ops:
  0.0 0.7 multiply_add_fusion
  0.7 0.1 copy.19
  0.8 0.8 copy.13
  1.6 0.7 reshape.37.owner_r
  2.2 0.8 copy.14
  3.0 0.7 reshape.38.local_r
  3.7 0.7 reshape.44.local_c
  4.4 0.7 reshape.43.owner_c
  5.1 0.7 broadcast_bitcast_fusion.ids
  5.8 39.4 %spread.1 = (bf16[2,4,32,64,128]{4,3,2,1,0:T(8,128)(2,1)}, bf16[2,32,128,128]{3,2,1,0:T(8,128)(2,1)}, bf16[16,2,32,128]{3,2,1,0:T(8,128)(2,1)}, bf16[8,1024,128]...) custom-call(bf16[32,512,128]{2,1,0:T(8,128)(2,1)} %bitcast.7, bf16[32,512,128]{2,1,0:T(8,128)(2,1)} %bitcast.8, ...), custom_call_target="tpu_custom_call" | custom-call | tf_op jit(solution)/shard_map/spread/pallas_call | solution.py:284
  45.1 60.3 %pick.1 = bf16[32,256,128]{2,1,0:T(8,128)(2,1)} custom-call(s32[4,8,128]{2,1,0:T(8,128)} %get-tuple-element.11.tabs, s32[8,128]{1,0:T(8,128)} %get-tuple-element.12.pos, s32[256,5]{1,0:T(8,128)} %broadcast_bitcast_fusion.ids, bf16[2,4,32,64,128]{4,3,2,1,0:T(8,128)(2,1)} %get-tuple-element.13.rows, bf16[2,32,128,128]{3,2,1,0:T(8,128)(2,1)} %get-tuple-element.14.own, ...), custom_call_target="tpu_custom_call" | custom-call | tf_op jit(solution)/shard_map/pick/pallas_call | solution.py:502
  105.5 4.4 %copy.21 = bf16[4096,2,128]{2,1,0:T(2,128)(2,1)} copy(bf16[4096,2,128]{2,1,0:T(2,128)(2,1)} %bitcast.6) | data formatting | bytes 4194304
  (2 shorter events, 0.0 us)

commit v3 on v2

--- a/solution.py
+++ b/solution.py
@@ -68,8 +68,8 @@
 
 
 def spread_kernel(
-    keys, values, queries, owner_r, local_r, owner_c, local_c,
-    rows, own, means, q_out, tabs, pos,
+    keys, values, queries, owner, local,
+    rows, own, means, q_out, q_later, tabs, pos,
     kv_in, q_in, half, row, both, q_st, tab_out, tab_in, pos_v, mean_a, mean_b,
     in_sem, a_send, a_recv, q_send, q_recv, t_send, t_recv, m_send, m_recv, x_send, x_recv, l_sem,
 ):
@@ -102,29 +102,28 @@
     chooser = jnp.where(in_row == out_row * KVH + kv, 1.0, 0.0).astype(BF16)
     my_half = pl.ds(at.core * HALF, HALF)
     gather, to_x = [], []
+    order = ((0, 1, 0), (1, 3, 2), (1, 1, 1), (0, 3, 3))
     for t in range(2):
         for p in range(parts):
             loads[t * parts + p].wait()
 
-            @pl.loop(p * per // 4, (p + 1) * per // 4)
+            @pl.loop(p * per // 8, (p + 1) * per // 8)
             def _(i, t=t):
-                for u in range(4):
-                    picked = jnp.dot(chooser, kv_in[t, i * 4 + u], preferred_element_type=F32)
+                for u in range(8):
+                    picked = jnp.dot(chooser, kv_in[t, i * 8 + u], preferred_element_type=F32)
                     picked = picked.astype(BF16)
-                    half[t, i * 4 + u] = picked
-                    both[t, i * 4 + u, my_half] = picked
-
-            if p == 1:
-                order = ((0, 1, 0), (1, 3, 2), (1, 1, 1), (0, 3, 3))
-                for part, k, n in order:
-                    where = pl.ds(part * per, per)
-                    gather.append(
-                        remote(
-                            half.at[t, where], row.at[t, at.a, where],
-                            a_send.at[t, n], a_recv.at[t, n], at.dev_a(k),
-                        )
+                    half[t, i * 8 + u] = picked
+                    both[t, i * 8 + u, my_half] = picked
+
+            for part, k, n in order[:1] if p == 0 else order[1:]:
+                where = pl.ds(part * per, per)
+                gather.append(
+                    remote(
+                        half.at[t, where], row.at[t, at.a, where],
+                        a_send.at[t, n], a_recv.at[t, n], at.dev_a(k),
                     )
-                start(gather[-4:])
+                )
+                gather[-1].start()
         to_x.append(
             remote(
                 both.at[t, :, my_half], both.at[t, :, my_half],
@@ -143,35 +142,51 @@
     order = jnp.where(in_row == (rest // 2) * 16 + pair * 2 + rest % 2, 1.0, 0.0).astype(BF16)
     chunks = q_in.shape[0] // (16 * step)
 
-    @pl.loop(0, chunks // 2)
-    def _(i):
-        for u in range(2):
-            first = pl.multiple_of((i * 2 + u) * 16 * step, 16 * step)
-            turned = jnp.dot(order, q_in[pl.ds(first, 16 * step)], preferred_element_type=F32)
-            turned = turned.astype(BF16)
-            place = pl.multiple_of((i * 2 + u) * 2 * step, 2 * step)
-            for h in range(HEADS):
-                q_st[h, pl.ds(place, 2 * step)] = turned[h * 2 * step : (h + 1) * 2 * step]
-
+    def turn(low, high):
+        @pl.loop(low // 4, high // 4)
+        def _(i):
+            for u in range(4):
+                first = pl.multiple_of((i * 4 + u) * 16 * step, 16 * step)
+                turned = jnp.dot(order, q_in[pl.ds(first, 16 * step)], preferred_element_type=F32)
+                turned = turned.astype(BF16)
+                place = pl.multiple_of((i * 4 + u) * 2 * step, 2 * step)
+                for h in range(HEADS):
+                    q_st[h, pl.ds(place, 2 * step)] = turned[h * 2 * step : (h + 1) * 2 * step]
+
+    turn(0, chunks // 2)
+    now = pl.ds(0, q_st.shape[1] // 2)
     asked = [
         remote(
-            q_st.at[(at.head + k) % HEADS], q_out.at[at.head],
+            q_st.at[(at.head + k) % HEADS, now], q_out.at[at.head],
             q_send.at[k - 1], q_recv.at[k - 1], at.dev_head(k),
         )
         for k in range(1, HEADS)
     ]
     start(asked)
-    own_q = pltpu.make_async_copy(q_st.at[at.head], q_out.at[at.head], l_sem.at[2])
+    own_q = pltpu.make_async_copy(q_st.at[at.head, now], q_out.at[at.head], l_sem.at[2])
     own_q.start()
-
-    ow_r, ow_c = owner_r[...], owner_c[...]
+    turn(chunks // 2, chunks)
+    later = pl.ds(q_st.shape[1] // 2, q_st.shape[1] // 2)
+    later_q = pltpu.make_async_copy(q_st.at[:, later], q_later, l_sem.at[24])
+    later_q.start()
+
+    lane = lax.broadcasted_iota(I32, (LISTED, LISTED), 1)
+    sub = lax.broadcasted_iota(I32, (LISTED, LISTED), 0)
+
+    def as_row(ref):
+        return jnp.concatenate([ref[r : r + 1] for r in range(REFINE)], axis=1)
+
+    def as_column(line):
+        spot = jnp.where(lane == sub, line.astype(F32), 0.0)
+        return jnp.sum(spot, axis=1, keepdims=True).astype(I32)
+
+    ow_r, lo_r = as_row(owner), as_row(local)
+    ow_c, lo_c = as_column(ow_r), as_column(lo_r)
     ar, br = ow_r // SIDE, ow_r % SIDE
     ac, bc = ow_c // SIDE, ow_c % SIDE
     br, bc = br + at.core * (ar - br), bc + at.core * (ac - bc)
     ac = ac + at.core * (ow_c % SIDE - ac)
-    id_r, id_c = ow_r * BLOCKS + local_r[...], ow_c * BLOCKS + local_c[...]
-    lane = lax.broadcasted_iota(I32, (LISTED, LISTED), 1)
-    sub = lax.broadcasted_iota(I32, (LISTED, LISTED), 0)
+    id_r, id_c = ow_r * BLOCKS + lo_r, ow_c * BLOCKS + lo_c
     twin = id_r == id_c
 
     def count(mask, axis):
@@ -182,12 +197,13 @@
     first_c = count(twin & (lane < sub), 1) == 0
     rank_c = count((bc == br) & (lane < sub) & first_r, 1)
     pos_r = jnp.sum(jnp.where(twin & first_c, rank_c, 0), axis=0, keepdims=True)
-    idx_c = ac * BLOCKS + local_c[...]
+    idx_c = ac * BLOCKS + lo_c
     for g in range(SIDE):
         wanted = first_c & (bc == g) & (rank_c == lane)
         table = jnp.sum(jnp.where(wanted, idx_c, 0), axis=0, keepdims=True)
         tab_out[g] = jnp.broadcast_to(table, (8, LISTED))
-    pos_v[...] = jnp.broadcast_to(br * LISTED + pos_r, (8, LISTED))
+    line = lax.broadcasted_iota(I32, (8, LISTED), 0)
+    pos_v[...] = jnp.where(line == 0, br * LISTED + pos_r, id_r)
     tables = [
         remote(
             tab_out.at[at.on_b(k)], tab_in.at[k], t_send.at[k - 1], t_recv.at[k - 1], at.dev_b(k)
@@ -269,7 +285,7 @@
         rows_out[-1].start()
     for copy in asked:
         copy.wait()
-    for copy in rows_out + mean_out + [own_q, pos_copy, own_out, tab_copy]:
+    for copy in rows_out + mean_out + [own_q, later_q, pos_copy, own_out, tab_copy]:
         copy.wait()
     for copy in gather + passed + to_x + tables + along_a + along_b:
         copy.wait_send()
@@ -287,12 +303,13 @@
             jax.ShapeDtypeStruct(row_shape, BF16),
             jax.ShapeDtypeStruct(own_shape, BF16),
             jax.ShapeDtypeStruct((SIDE * SIDE,) + mean_shape, BF16),
-            jax.ShapeDtypeStruct((HEADS, q_rows, HD), BF16),
+            jax.ShapeDtypeStruct((HEADS, q_rows // 2, HD), BF16),
+            jax.ShapeDtypeStruct((HEADS, q_rows // 2, HD), BF16),
             jax.ShapeDtypeStruct((SIDE, 8, LISTED), I32),
             jax.ShapeDtypeStruct((8, LISTED), I32),
         ),
-        in_specs=[hbm, hbm, hbm, vmem, vmem, vmem, vmem],
-        out_specs=(hbm,) * 6,
+        in_specs=[hbm, hbm, hbm, vmem, vmem],
+        out_specs=(hbm,) * 7,
         scratch_shapes=[
             pltpu.VMEM((2, BLOCKS, HALF * KVH, HD), BF16),
             pltpu.VMEM(queries.shape, BF16),
@@ -306,16 +323,13 @@
             pltpu.VMEM((SIDE,) + mean_shape, BF16),
             pltpu.VMEM((SIDE, SIDE) + mean_shape, BF16),
             DMA((5,)), DMA((2, 6)), DMA((2, 6)), DMA((HEADS - 1,)), DMA((HEADS - 1,)),
-            DMA((3,)), DMA((3,)), DMA((6,)), DMA((6,)), DMA((2,)), DMA((2,)), DMA((24,)),
+            DMA((3,)), DMA((3,)), DMA((6,)), DMA((6,)), DMA((2,)), DMA((2,)), DMA((25,)),
         ],
         compiler_params=pltpu.CompilerParams(
             collective_id=0, has_side_effects=True, vmem_limit_bytes=60 * MIB
         ),
         name="spread",
-    )(
-        keys, values, queries, owner.reshape(1, LISTED), local.reshape(1, LISTED),
-        owner.reshape(LISTED, 1), local.reshape(LISTED, 1),
-    )
+    )(keys, values, queries, owner, local)
 
 
 def scores(left, right):
@@ -323,20 +337,22 @@
 
 
 def pick_kernel(
-    cap, tabs, pos, ids, rows, own, means, q_hbm, out,
+    cap, tabs, pos, rows, own, means, q_first, q_later, out,
     row_k, row_v, both, mean, q, sendbuf, recv_k, recv_v, far, weights, base, q_mean, c_max, c_sum, c_val, o_st,
-    in_sem, s_send, s_recv, x_send, x_recv, o_sem,
+    in_sem, s_send, s_recv, x_send, x_recv, q_send, q_recv, o_sem,
 ):
     at = Place()
     row, recv = (row_k, row_v), (recv_k, recv_v)
+    early, late = pl.ds(0, q.shape[1] // 2), pl.ds(q.shape[1] // 2, q.shape[1] // 2)
     loads = [pltpu.make_async_copy(rows.at[t], row[t], in_sem.at[t]) for t in range(2)]
     loads += [
-        pltpu.make_async_copy(q_hbm, q, in_sem.at[2]),
+        pltpu.make_async_copy(q_first, q.at[:, early], in_sem.at[2]),
         pltpu.make_async_copy(means, mean, in_sem.at[3]),
         pltpu.make_async_copy(own, both, in_sem.at[4]),
+        pltpu.make_async_copy(q_later.at[at.head], q.at[at.head, late], in_sem.at[5]),
     ]
     start(loads)
-    greet([at.dev_b(k) for k in range(1, SIDE)] + [at.sibling])
+    greet([at.dev_b(k) for k in range(1, SIDE)] + [at.dev_head(k) for k in range(1, HEADS)])
 
     picks = [[], []]
     offsets = (2, 1, 3)
@@ -366,6 +382,14 @@
                 recv[t][at.b, i * 8 + u] = blocks[tabs[0, 0, i * 8 + u]]
 
     collect(0)
+    asked = [
+        remote(
+            q_later.at[(at.head + k) % HEADS], q.at[at.head, late],
+            q_send.at[k - 1], q_recv.at[k - 1], at.dev_head(k),
+        )
+        for k in range(1, HEADS)
+    ]
+    start(asked)
     collect(1)
 
     to_log2 = math.log2(math.e)
@@ -373,8 +397,10 @@
     which = lax.broadcasted_iota(I32, (8, ROWS), 0)
     column = lax.broadcasted_iota(I32, (8, ROWS), 1)
     parity = jnp.where(which == column % 2, 1.0 / BLK, 0.0).astype(BF16)
-    loads[2].wait()
-    loads[3].wait()
+    for n in (2, 3, 5):
+        loads[n].wait()
+    for copy in asked:
+        copy.wait_recv()
     per_owner = q.shape[1] // ROWS
 
     def q_rows(i):
@@ -401,14 +427,18 @@
         low = (rest - mid.astype(F32)).astype(BF16)
         coarse = scores(high, key_means) + scores(mid, key_means) + scores(low, key_means)
         coarse = coarse * scale + math.log2(BLK)
-        number = lax.broadcasted_iota(I32, coarse.shape, 1)
-        listed = ids[pl.ds(pl.multiple_of(i * group * 8, group * 8), group * 8)]
-        gone = number == listed[:, 0:1]
-        for r in range(1, REFINE + 1):
-            gone = gone | (number == listed[:, r : r + 1])
-        coarse = jnp.where(gone, -1e30, coarse)
+        number = lax.broadcasted_iota(I32, (8, total_blocks), 1)
+        kept = []
+        for u in range(group):
+            block = i * group + u
+            gone = number == at.seq * BLOCKS + block
+            for r in range(REFINE):
+                gone = gone | (number == pos[1, r * BLOCKS + block])
+            kept.append(jnp.where(gone, 0.0, 1.0))
+        kept = jnp.concatenate(kept, axis=0) > 0.0
+        coarse = jnp.where(kept, coarse, -1e30)
         top = jnp.max(coarse, axis=1, keepdims=True)
-        part = jnp.where(gone, 0.0, jnp.exp2(coarse - top))
+        part = jnp.where(kept, jnp.exp2(coarse - top), 0.0)
         c_max[where] = jnp.broadcast_to(top, (group * 8, HD)).reshape(group, 8, HD)
         total = jnp.sum(part, axis=1, keepdims=True)
         c_sum[where] = jnp.broadcast_to(total, (group * 8, HD)).reshape(group, 8, HD)
@@ -422,7 +452,7 @@
 
     my_half = pl.ds(at.core * HALF, HALF)
     pieces = 4
-    piece = LISTED // pieces
+    piece, blocks_piece = LISTED // pieces, BLOCKS // pieces
 
     def listed_blocks(t):
         for copy in picks[t]:
@@ -430,12 +460,13 @@
         copies = []
         for p in range(pieces):
 
-            @pl.loop(0, piece // 8)
-            def _(i, p=p):
-                for u in range(8):
-                    e = p * piece + i * 8 + u
-                    place = pos[0, e]
-                    far[t, e, my_half] = recv[t][place // LISTED, place % LISTED]
+            @pl.loop(p * blocks_piece // 2, (p + 1) * blocks_piece // 2)
+            def _(j):
+                for u in range(2):
+                    for r in range(REFINE):
+                        i = j * 2 + u
+                        place = pos[0, r * BLOCKS + i]
+                        far[t, i * REFINE + r, my_half] = recv[t][place // LISTED, place % LISTED]
 
             ref = far.at[t, pl.ds(p * piece, piece), my_half]
             copies.append(
@@ -450,14 +481,13 @@
         return jnp.where(odd, ref[i, 1:2, :width], ref[i, 0:1, :width])
 
     key_copies = listed_blocks(0)
-    blocks_piece = BLOCKS // pieces
     for p in range(pieces):
         key_copies[p].wait_recv()
 
-        @pl.loop(p * blocks_piece // 2, (p + 1) * blocks_piece // 2)
+        @pl.loop(p * blocks_piece // 4, (p + 1) * blocks_piece // 4)
         def _(j):
-            for u in range(2):
-                i = j * 2 + u
+            for u in range(4):
+                i = j * 4 + u
                 block_keys = jnp.concatenate(
                     [both[0, i], far[0, pl.ds(i * REFINE, REFINE)].reshape(REFINE * BLK, HD)], axis=0
                 )
@@ -476,10 +506,10 @@
     for p in range(pieces):
         value_copies[p].wait_recv()
 
-        @pl.loop(p * blocks_piece // 2, (p + 1) * blocks_piece // 2)
+        @pl.loop(p * blocks_piece // 4, (p + 1) * blocks_piece // 4)
         def _(j):
-            for u in range(2):
-                i = j * 2 + u
+            for u in range(4):
+                i = j * 4 + u
                 block_values = jnp.concatenate(
                     [both[1, i], far[1, pl.ds(i * REFINE, REFINE)].reshape(REFINE * BLK, HD)], axis=0
                 )
@@ -492,24 +522,24 @@
 
     for copy in outs:
         copy.wait()
-    for copy in key_copies + value_copies + picks[1]:
+    for copy in key_copies + value_copies + picks[1] + asked:
         copy.wait_send()
 
 
-def pick(cap, collective_id, rows, own, means, q, tabs, pos, ids):
-    smem, vmem = pl.BlockSpec(memory_space=pltpu.SMEM), pl.BlockSpec(memory_space=pltpu.VMEM)
-    hbm = pl.BlockSpec(memory_space=pl.ANY)
+def pick(cap, collective_id, rows, own, means, q_first, q_later, tabs, pos):
+    smem, hbm = pl.BlockSpec(memory_space=pltpu.SMEM), pl.BlockSpec(memory_space=pl.ANY)
+    q_shape = (HEADS, 2 * q_first.shape[1], HD)
     return pl.pallas_call(
         functools.partial(pick_kernel, cap),
         out_shape=jax.ShapeDtypeStruct((BLOCKS, ROWS, HD), BF16),
-        in_specs=[smem, smem, vmem, hbm, hbm, hbm, hbm],
+        in_specs=[smem, smem, hbm, hbm, hbm, hbm, hbm],
         out_specs=hbm,
         scratch_shapes=[
             pltpu.VMEM(rows.shape[1:], BF16),
             pltpu.VMEM(rows.shape[1:], BF16),
             pltpu.VMEM(own.shape, BF16),
             pltpu.VMEM(means.shape, BF16),
-            pltpu.VMEM(q.shape, BF16),
+            pltpu.VMEM(q_shape, BF16),
             pltpu.VMEM((2, SIDE - 1, cap, HALF, HD), BF16),
             pltpu.VMEM((SIDE, cap, HALF, HD), BF16),
             pltpu.VMEM((SIDE, cap, HALF, HD), BF16),
@@ -521,29 +551,57 @@
             pltpu.VMEM((BLOCKS, 8, HD), F32),
             pltpu.VMEM((BLOCKS, 8, HD), F32),
             pltpu.VMEM((BLOCKS, ROWS, HD), BF16),
-            DMA((5,)), DMA((2, 3)), DMA((2, 3)), DMA((2, 4)), DMA((2, 4)), DMA((4,)),
+            DMA((6,)), DMA((2, 3)), DMA((2, 3)), DMA((2, 4)), DMA((2, 4)),
+            DMA((HEADS - 1,)), DMA((HEADS - 1,)), DMA((4,)),
         ],
         compiler_params=pltpu.CompilerParams(
             collective_id=collective_id, has_side_effects=True, vmem_limit_bytes=60 * MIB
         ),
         name="pick",
-    )(tabs, pos, ids, rows, own, means, q)
+    )(tabs, pos, rows, own, means, q_first, q_later)
+
+
+def hand_on_kernel(src, dst, held, in_sem, out_sem):
+    parts = in_sem.shape[0]
+    per = BLOCKS // parts
+    where = [pl.ds(p * per, per) for p in range(parts)]
+    inward = [
+        pltpu.make_async_copy(src.at[w], held.at[w], in_sem.at[p]) for p, w in enumerate(where)
+    ]
+    outward = [
+        pltpu.make_async_copy(held.at[w], dst.at[w], out_sem.at[p]) for p, w in enumerate(where)
+    ]
+    start(inward)
+    for before, after in zip(inward, outward):
+        before.wait()
+        after.start()
+    for copy in outward:
+        copy.wait()
+
+
+def hand_on(result):
+    hbm = pl.BlockSpec(memory_space=pl.ANY)
+    return pl.pallas_call(
+        hand_on_kernel,
+        out_shape=jax.ShapeDtypeStruct(result.shape, result.dtype),
+        in_specs=[hbm],
+        out_specs=hbm,
+        scratch_shapes=[pltpu.VMEM(result.shape, result.dtype), DMA((8,)), DMA((8,))],
+        compiler_params=pltpu.CompilerParams(vmem_limit_bytes=60 * MIB),
+        name="hand_on",
+    )(result)
 
 
 def on_device(queries, keys, values, refine_owner, refine_local):
-    first = lax.axis_index("seq") * BLOCKS
-    own_ids = (first + jnp.arange(BLOCKS, dtype=I32))[:, None]
-    ids = jnp.concatenate([own_ids, refine_owner * BLOCKS + refine_local], axis=1)
-    ids = jnp.repeat(ids, 8, axis=0)
-    rows, own, means, q, tabs, pos = spread(
+    rows, own, means, q_first, q_later, tabs, pos = spread(
         keys.reshape(BLOCKS, BLK * KVH, HD),
         values.reshape(BLOCKS, BLK * KVH, HD),
         queries.reshape(-1, HD),
-        refine_owner,
-        refine_local,
+        refine_owner.T,
+        refine_local.T,
     )
-    out = pick(64, 1, rows, own, means, q, tabs, pos, ids)
-    return out.reshape(BLOCKS * BLK, 2, HD)
+    out = pick(64, 1, rows, own, means, q_first, q_later, tabs, pos)
+    return hand_on(out).reshape(BLOCKS * BLK, 2, HD)
 
 
 def solution(mesh):

time: 110 us -> 99.5 us (0.905)
  local copies, waits for them, and re-layouts: 9.47 us -> 0 us
    unnamed x3 -> x0, local copies, waits for them, and re-layouts: 5.96 us -> none
    pallas_call x1, Pallas kernels: 39.4 us -> 35.5 us  [spread(): pl.pallas_call(spread_kernel, out_shape=(jax.ShapeDtypeStruct(row_shape,...]
    reshape x5 -> x0, local copies, waits for them, and re-layouts: 3.42 us -> none  [the longest x1 0.71 us: spread(): owner.reshape(LISTED, 1)]
    pallas_call x0 -> x1, Pallas kernels: none -> 2.39 us  [hand_on(): pl.pallas_call(hand_on_kernel, out_shape=jax.ShapeDtypeStruct(result.shap...]
where the time goes in v3:
time: 99.5 us; the launch traced here: 99.3 us
  Pallas kernels  99.3 us (100%)
    pallas_call x1, Pallas kernels, pick(): pl.pallas_call(functools.partial(pick_kernel, cap), out_shape=jax.ShapeDt...  61.4 us
    pallas_call x1, Pallas kernels, spread(): pl.pallas_call(spread_kernel, out_shape=(jax.ShapeDtypeStruct(row_shape,...  35.5 us
    pallas_call x1, Pallas kernels, hand_on(): pl.pallas_call(hand_on_kernel, out_shape=jax.ShapeDtypeStruct(result.shap...  2.39 us

profile of v3, /device:TPU:1, one launch (start us, length us, event | category | flops | bytes accessed | tf_op | source)
XLA Modules:
  0.0 99.3 jit_solution(4110198761614069411)
XLA Ops:
  0.0 35.5 %spread.1 = (bf16[2,4,32,64,128]{4,3,2,1,0:T(8,128)(2,1)}, bf16[2,32,128,128]{3,2,1,0:T(8,128)(2,1)}, bf16[16,2,32,128]{3,2,1,0:T(8,128)(2,1)}, bf16[8,512,128]{...) custom-call(bf16[32,512,128]{2,1,0:T(8,128)(2,1)} %bitcast.6, ...), custom_call_target="tpu_custom_call" | custom-call | tf_op jit(solution)/shard_map/spread/pallas_call | solution.py:300
  35.5 61.4 %pick.1.src = bf16[32,256,128]{2,1,0:T(8,128)(2,1)} custom-call(s32[4,8,128]{2,1,0:T(8,128)} %get-tuple-element.12.tabs, s32[8,128]{1,0:T(8,128)} %get-tuple-element.13.pos, bf16[2,4,32,64,128]{4,3,2,1,0:T(8,128)(2,1)} %get-tuple-element.14.rows, bf16[2,32,128,128]{3,2,1,0:T(8,128)(2,1)} %get-tuple-element.15.own, ...), custom_call_target="tpu_custom_call" | custom-call | tf_op jit(solution)/shard_map/pick/pallas_call | solution.py:532
  96.9 2.4 %hand_on.1 = bf16[32,256,128]{2,1,0:T(8,128)(2,1)} custom-call(bf16[32,256,128]{2,1,0:T(8,128)(2,1)} %pick.1.src), custom_call_target="tpu_custom_call" | custom-call | tf_op jit(solution)/shard_map/hand_on/pallas_call | solution.py:584
